TPU v7x, 256 devices: a whole 4x4x8 slice. The times are simulated.
256 devices in a mesh: loop: 16 (over y, x), dp: 16 (over z, core).
Axes of the slice: x: 4, y: 4, z: 8, core: 2. Of those that a mesh axis runs over, the one named last changes fastest.
Arguments:
- tokens: bfloat16 [3584, 8192], P('dp', 'loop'), may hold values from -8 to 8
- weight: bfloat16 [8192, 14336], P('loop', 'dp'), as said below
- rounding: float32 [8192, 14336], P('loop', 'dp'), may hold values from -6 to 6
- floor_codes: int32 [8192, 14336], P('loop', 'dp'), may hold values from -1 to 15
- scale_codes: int32 [14336], P('dp'), may hold values from 12 to 15
- zero_codes: int32 [14336], P('dp'), may hold values from 0 to 15
- block_mask: int32 [128, 224], P('loop', 'dp'), may hold values from 0 to 1, as said below
Outputs:
- refined: float32 [8192, 14336], P('loop', 'dp')
Inputs may be any that keep to these rules, and one draw needn't show every extreme that they name: weight equals scales times (floor_codes - zero_point + a fraction in [0, 1)), then is rounded to bfloat16. `block_mask`: the share of surviving blocks differs between column blocks.
All inputs are finite; a program needn't handle non-finite values.
Results may differ from a plain program's by a relative error of at most 0.019.
Values may be sent and summed in bfloat16 or wider, within the bound.
A program may use at most 128 MiB of HBM per device.

v0:
```python
import jax
import jax.numpy as jnp
from jax import lax
from jax.sharding import PartitionSpec as P

BLOCK = 64
ITERS = 2


step_rate = 20.0
reg_weight = 0.05
base_scale = 0.02


def expand(block_mask):
    row_blocks, col_blocks = block_mask.shape
    spread = jnp.broadcast_to(block_mask[:, None, :, None], (row_blocks, BLOCK, col_blocks, BLOCK))
    return spread.reshape(row_blocks * BLOCK, col_blocks * BLOCK).astype(jnp.float32)


def token_product(token_rows, scaled_err):
    return lax.dot_general(
        token_rows, scaled_err, (((0,), (0,)), ((), ())), preferred_element_type=jnp.float32
    )


def per_device(tokens, weight, rounding, floor_codes, scale_codes, zero_codes, block_mask):
    gathered = lax.all_gather(tokens, "dp", axis=0, tiled=True)
    token_count = gathered.shape[0]
    scales = base_scale * jnp.exp2(scale_codes.astype(jnp.float32) * 0.25)
    zero_point = zero_codes.astype(jnp.float32)
    kept_mask = expand(block_mask)
    floors = floor_codes.astype(jnp.float32)
    in_range = ((floor_codes >= 0) & (floor_codes <= 14)).astype(jnp.float32)
    target = weight.astype(jnp.float32)
    for iteration in range(ITERS):
        relaxed = jax.nn.sigmoid(rounding)
        levels = jnp.clip(floors + relaxed, 0.0, 15.0)
        w_delta = (kept_mask * (scales[None, :] * (levels - zero_point[None, :]) - target)).astype(
            jnp.bfloat16
        )
        partial_sum = jnp.dot(gathered, w_delta, preferred_element_type=jnp.float32)
        residual = lax.psum(partial_sum.astype(jnp.bfloat16), "loop").astype(jnp.float32)
        scaled_err = (2.0 / token_count * residual).astype(jnp.bfloat16)
        gradient = token_product(gathered, scaled_err)
        centered = 2.0 * relaxed - 1.0
        descent = gradient * scales[None, :] * in_range - reg_weight * 8.0 * centered**3
        rounding = rounding - step_rate * kept_mask * descent * relaxed * (1.0 - relaxed)
    return rounding


def solution(mesh):
    placed = (
        P("dp", "loop"),
        P("loop", "dp"),
        P("loop", "dp"),
        P("loop", "dp"),
        P("dp"),
        P("dp"),
        P("loop", "dp"),
    )
    return jax.shard_map(
        per_device, mesh=mesh, in_specs=placed, out_specs=P("loop", "dp"), check_vma=False
    )
```

profile of v0, /device:TPU:2, one launch (start us, length us, event | category | flops | bytes accessed | tf_op | source)
XLA Modules:
  0.0 364.1 jit_solution(10741293267602168995)
XLA Ops:
  6.5 0.0 all-gather.2.cloned.1.call-start
  6.5 0.7 all-gather.2.cloned.1.call-update
  7.3 0.0 all-reduce.3.cloned.1.call-start
  7.3 0.7 convert_element_type.50
  8.0 0.1 copy.8
  8.1 2.1 broadcast_in_dim.2
  10.2 4.4 %convert_element_type.51 = f32[512,896]{0,1:T(8,128)} reshape(f32[8,64,14,64]{1,0,3,2:T(8,128)} %broadcast_in_dim.2) | data formatting | bytes 3670016 | tf_op jit(solution)/shard_map/convert_element_type | solution.py:18
  14.6 1.8 copy.9
  16.4 0.0 copy-start.1
  16.4 0.0 copy-start.3
  16.4 2.8 copy.14
  19.2 0.0 copy-done.1
  19.2 1.3 copy.13
  20.5 0.0 copy-done.3
  20.5 0.0 copy-done.4
  20.5 33.2 %all-gather.2.cloned.1.call-done = bf16[3584,512]{1,0:T(8,128)(2,1)} async-done(((bf16[224,512]{1,0:T(8,128)(2,1)}), bf16[3584,512]{1,0:T(8,128)(2,1)}) %all-gather.2.cloned.1.call-update) | async-done | bytes 3670032 | tf_op jit(solution)/shard_map/all_gather | solution.py:28
  53.8 10.1 %fusion.4 = bf16[3584,896]{0,1:T(8,128)(2,1)} fusion(bf16[3584,512]{1,0:T(8,128)(2,1)} %all-gather.2.cloned.1.call-done, f32[512,896]{0,1:T(8,128)} %convert_element_type.51, bf16[512,896]{0,1:T(8,128)(2,1)} %copy.13, s32[512,896]{0,1:T(8,128)S(1)} %copy.9, f32[512,896]{0,1:T(8,128)} %copy.14, f32[896]{0:T(1024)S(1)} %convert_element_type.54, ...), kind=kOutput, calls=%fused_computation.8 | convolution fusion | flops 3297050624 | bytes 16522240 | tf_op jit(solution)/shard_map/dot_general | solution.py:42
  63.8 0.0 all-reduce.3.cloned.1.call-update
  63.8 0.2 all-reduce.5.cloned.1.call-start
  64.1 0.4 compare_and_fusion
  64.4 0.0 copy-start.2
  64.5 131.7 %all-reduce.3.cloned.1.call-done = bf16[3584,896]{0,1:T(8,128)(2,1)} async-done(((bf16[3584,896]{0,1:T(8,128)(2,1)}), bf16[3584,896]{0,1:T(8,128)(2,1)}) %all-reduce.3.cloned.1.call-update) | async-done | bytes 6422544 | tf_op jit(solution)/shard_map/psum | solution.py:43
  196.1 9.5 %fusion.15 = f32[512,896]{0,1:T(8,128)S(1)} fusion(f32[512,896]{0,1:T(8,128)} %copy.14, pred[512,896]{0,1:T(32,128)(4,1)S(1)} %compare_and_fusion, f32[512,896]{0,1:T(8,128)} %convert_element_type.51, bf16[3584,512]{1,0:T(8,128)(2,1)} %all-gather.2.cloned.1.call-done, bf16[3584,896]{0,1:T(8,128)(2,1)} %all-reduce.3.cloned.1.call-done, ...), kind=kOutput, calls=%fused_computation.23 | convolution fusion | flops 3305766912 | bytes 16059904 | tf_op jit(solution)/shard_map/dot_general | solution.py:22
  205.6 0.0 copy-start.6
  205.7 1.2 copy-done.6
  206.9 0.0 copy-done.2
  206.9 0.0 copy-done
  206.9 6.2 %fusion.5 = bf16[3584,896]{0,1:T(8,128)(2,1)} fusion(bf16[3584,512]{1,0:T(8,128)(2,1)S(1)} %copy-done.5, f32[512,896]{0,1:T(8,128)S(1)} %copy-done, bf16[512,896]{0,1:T(8,128)(2,1)S(1)} %copy-done.2, s32[512,896]{0,1:T(8,128)S(1)} %copy.9, f32[512,896]{0,1:T(8,128)S(1)} %fusion.15, f32[896]{0:T(1024)S(1)} %convert_element_type.54, ...), kind=kOutput, calls=%fused_computation.9 | convolution fusion | flops 3297050624 | bytes 16522240 | tf_op jit(solution)/shard_map/dot_general | solution.py:42
  213.0 0.0 all-reduce.5.cloned.1.call-update
  213.1 133.5 %all-reduce.5.cloned.1.call-done = bf16[3584,896]{0,1:T(8,128)(2,1)} async-done(((bf16[3584,896]{0,1:T(8,128)(2,1)}), bf16[3584,896]{0,1:T(8,128)(2,1)}) %all-reduce.5.cloned.1.call-update) | async-done | bytes 6422544 | tf_op jit(solution)/shard_map/psum | solution.py:43
  346.5 9.4 %fusion.21 = f32[512,896]{0,1:T(8,128)S(1)} fusion(f32[512,896]{0,1:T(8,128)} %copy-done.6, pred[512,896]{0,1:T(32,128)(4,1)S(1)} %compare_and_fusion, f32[512,896]{0,1:T(8,128)} %convert_element_type.51, bf16[3584,512]{1,0:T(8,128)(2,1)} %all-gather.2.cloned.1.call-done, bf16[3584,896]{0,1:T(8,128)(2,1)} %all-reduce.5.cloned.1.call-done, ...), kind=kOutput, calls=%fused_computation.29 | convolution fusion | flops 3305766912 | bytes 16059904 | tf_op jit(solution)/shard_map/dot_general | solution.py:22
  355.9 1.7 copy.15
  (6 shorter events, 0.0 us)
Async XLA Ops:
  6.5 47.2 %all-gather.2.cloned.1.call-start = ((), (), s32[]{:S(2)}) async-start(), calls=%async_computation | async-start | bytes 3899392 | tf_op jit(solution)/shard_map/all_gather | solution.py:28
  7.3 188.9 %all-reduce.3.cloned.1.call-start = ((), (), s32[]{:S(2)}) async-start(), calls=%async_computation.1 | async-start | bytes 12845056 | tf_op jit(solution)/shard_map/psum | solution.py:43
  16.4 2.8 copy-start.1
  16.4 4.1 %copy-start.3 = (s32[896]{0:T(1024)S(1)}, s32[896]{0:T(1024)}, u32[]{:S(2)}) copy-start(s32[896]{0:T(1024)} %param.12) | copy-start | bytes 10756
  19.2 1.3 copy-start.4
  63.8 282.7 %all-reduce.5.cloned.1.call-start = ((), (), s32[]{:S(2)}) async-start(), calls=%async_computation.2 | async-start | bytes 12845056 | tf_op jit(solution)/shard_map/psum | solution.py:43
  64.4 142.4 %copy-start.2 = (bf16[512,896]{0,1:T(8,128)(2,1)S(1)}, bf16[512,896]{0,1:T(8,128)(2,1)}, u32[]{:S(2)}) copy-start(bf16[512,896]{0,1:T(8,128)(2,1)} %copy.13) | copy-start | bytes 2752516
  196.1 10.8 %copy-start = (f32[512,896]{0,1:T(8,128)S(1)}, f32[512,896]{0,1:T(8,128)}, u32[]{:S(2)}) copy-start(f32[512,896]{0,1:T(8,128)} %convert_element_type.51) | copy-start | bytes 5505028
  196.1 10.8 %copy-start.5 = (bf16[3584,512]{1,0:T(8,128)(2,1)S(1)}, bf16[3584,512]{1,0:T(8,128)(2,1)}, u32[]{:S(2)}) copy-start(bf16[3584,512]{1,0:T(8,128)(2,1)} %all-gather.2.cloned.1.call-done) | copy-start | bytes 11010052
  205.6 1.2 copy-start.6
Sparse Core Ops, SparseCore 0:
  9.2 44.5 all-gather.1
  64.0 132.1 all-reduce.2
  213.2 133.3 all-reduce.4
where the time goes:
time: 365 us; the launch traced here: 364 us
  waiting for transfers between devices  299 us (82%)
  matrix products  35.1 us (10%)
  local copies, waits for them, and re-layouts  15.4 us (4%)
  between operations  13.2 us (4%)
    psum x2, waiting for transfers between devices, per_device(): lax.psum(partial_sum.astype(jnp.bfloat16), 'loop').astype(jnp.float32)  265 us
    all_gather x1, waiting for transfers between devices, per_device(): gathered = lax.all_gather(tokens, 'dp', axis=0, tiled=True)  33.2 us
    dot_general x2, matrix products, token_product(): lax.dot_general(token_rows, scaled_err, (((0,), (0,)), ((), ())), preferr...  18.9 us
    dot_general x2, matrix products, per_device(): partial_sum = jnp.dot(gathered, w_delta, preferred_element_type=jnp.float32)  16.2 us
  transfers between devices with their start and end apart: 3, of which 3 were waited for; matrix products, arithmetic and copies ran while one was open for 4% of the time, Pallas kernels for 0%

commit v1 on v0

--- a/solution.py
+++ b/solution.py
@@ -1,6 +1,7 @@
 import jax
 import jax.numpy as jnp
 from jax import lax
+from jax.sharding import Mesh
 from jax.sharding import PartitionSpec as P
 
 BLOCK = 64
@@ -25,7 +26,8 @@
 
 
 def per_device(tokens, weight, rounding, floor_codes, scale_codes, zero_codes, block_mask):
-    gathered = lax.all_gather(tokens, "dp", axis=0, tiled=True)
+    gathered = lax.all_gather(tokens, ("z", "core"), axis=0, tiled=True)
+    gathered = lax.all_gather(gathered, "y", axis=1, tiled=True)
     token_count = gathered.shape[0]
     scales = base_scale * jnp.exp2(scale_codes.astype(jnp.float32) * 0.25)
     zero_point = zero_codes.astype(jnp.float32)
@@ -39,10 +41,13 @@
         w_delta = (kept_mask * (scales[None, :] * (levels - zero_point[None, :]) - target)).astype(
             jnp.bfloat16
         )
-        partial_sum = jnp.dot(gathered, w_delta, preferred_element_type=jnp.float32)
-        residual = lax.psum(partial_sum.astype(jnp.bfloat16), "loop").astype(jnp.float32)
+        w_tall = lax.all_to_all(w_delta, "y", split_axis=1, concat_axis=0, tiled=True)
+        partial_sum = jnp.dot(gathered, w_tall, preferred_element_type=jnp.float32)
+        residual = lax.psum(partial_sum.astype(jnp.bfloat16), "x").astype(jnp.float32)
         scaled_err = (2.0 / token_count * residual).astype(jnp.bfloat16)
-        gradient = token_product(gathered, scaled_err)
+        grad_tall = token_product(gathered, scaled_err).astype(jnp.bfloat16)
+        gradient = lax.all_to_all(grad_tall, "y", split_axis=0, concat_axis=1, tiled=True)
+        gradient = gradient.astype(jnp.float32)
         centered = 2.0 * relaxed - 1.0
         descent = gradient * scales[None, :] * in_range - reg_weight * 8.0 * centered**3
         rounding = rounding - step_rate * kept_mask * descent * relaxed * (1.0 - relaxed)
@@ -50,15 +55,17 @@
 
 
 def solution(mesh):
+    fine = Mesh(mesh.devices.reshape(4, 4, 8, 2), ("y", "x", "z", "core"))
+    loop, dp = ("y", "x"), ("z", "core")
     placed = (
-        P("dp", "loop"),
-        P("loop", "dp"),
-        P("loop", "dp"),
-        P("loop", "dp"),
-        P("dp"),
-        P("dp"),
-        P("loop", "dp"),
+        P(dp, loop),
+        P(loop, dp),
+        P(loop, dp),
+        P(loop, dp),
+        P(dp),
+        P(dp),
+        P(loop, dp),
     )
     return jax.shard_map(
-        per_device, mesh=mesh, in_specs=placed, out_specs=P("loop", "dp"), check_vma=False
+        per_device, mesh=fine, in_specs=placed, out_specs=P(loop, dp), check_vma=False
     )

time: 365 us -> 420 us (1.15)
  blocking collectives: 0 us -> 78.3 us
  waiting for transfers between devices: 299 us -> 261 us
  other arithmetic: 1.06 us -> 9.91 us
  matrix products: 35.1 us -> 40 us
    psum x2, waiting for transfers between devices: 265 us -> 110 us  [per_device(): lax.psum(partial_sum.astype(jnp.bfloat16), 'x').astype(jnp.float32)]
    all_gather x1 -> x2, waiting for transfers between devices: 33.2 us -> 150 us  [the longest x1 104 us: per_device(): gathered = lax.all_gather(gathered, 'y', axis=1, tiled=True)]
    all_to_all x0 -> x4, blocking collectives: none -> 78.3 us  [the longest x2 43.2 us: per_device(): lax.all_to_all(w_delta, 'y', split_axis=1, concat_axis=0, tiled=True)]
    convert_element_type x0 -> x2, other arithmetic: none -> 6.09 us  [per_device(): (kept_mask * (scales[None, :] * (levels - zero_point[None, :]) - target))...]
    dot_general x2, matrix products: 16.2 us -> 21.6 us  [per_device(): partial_sum = jnp.dot(gathered, w_tall, preferred_element_type=jnp.float32)]
  transfers between devices with their start and end apart: 3 -> 4, of which waited for: 3 -> 4; matrix products, arithmetic and copies ran while one was open for 4% -> 4% of each run, Pallas kernels for 0% -> 0%
where the time goes in v1:
time: 420 us; the launch traced here: 419 us
  waiting for transfers between devices  261 us (62%)
  blocking collectives  78.3 us (19%)
  matrix products  40 us (10%)
  local copies, waits for them, and re-layouts  16.3 us (4%)
  between operations  13.3 us (3%)
  other arithmetic  9.91 us (2%)
    psum x2, waiting for transfers between devices, per_device(): lax.psum(partial_sum.astype(jnp.bfloat16), 'x').astype(jnp.float32)  110 us
    all_gather x1, waiting for transfers between devices, per_device(): gathered = lax.all_gather(gathered, 'y', axis=1, tiled=True)  104 us
    all_gather x1, waiting for transfers between devices, per_device(): gathered = lax.all_gather(tokens, ('z', 'core'), axis=0, tiled=True)  46.5 us
    all_to_all x2, blocking collectives, per_device(): lax.all_to_all(w_delta, 'y', split_axis=1, concat_axis=0, tiled=True)  43.2 us
    all_to_all x2, blocking collectives, per_device(): lax.all_to_all(grad_tall, 'y', split_axis=0, concat_axis=1, tiled=True)  35.2 us
    dot_general x2, matrix products, per_device(): partial_sum = jnp.dot(gathered, w_tall, preferred_element_type=jnp.float32)  21.6 us
    dot_general x2, matrix products, token_product(): lax.dot_general(token_rows, scaled_err, (((0,), (0,)), ((), ())), preferr...  18.4 us
  transfers between devices with their start and end apart: 4, of which 4 were waited for; matrix products, arithmetic and copies ran while one was open for 4% of the time, Pallas kernels for 0%

profile of v1, /device:TPU:2, one launch (start us, length us, event | category | flops | bytes accessed | tf_op | source)
XLA Modules:
  0.0 418.8 jit_solution(2932605341265090691)
XLA Ops:
  6.5 0.7 all-gather.3.cloned.1.call-update
  7.3 0.0 all-gather.5.cloned.1.call-start
  7.3 46.5 %all-gather.3.cloned.1.call-done = bf16[3584,512]{1,0:T(8,128)(2,1)} async-done(((bf16[224,512]{1,0:T(8,128)(2,1)}), bf16[3584,512]{1,0:T(8,128)(2,1)}) %all-gather.3.cloned.1.call-update) | async-done | bytes 3670032 | tf_op jit(solution)/shard_map/all_gather | solution.py:29
  53.8 0.0 all-reduce.3.cloned.1.call-start
  53.8 0.6 copy-done.6
  54.5 0.1 copy.10
  54.5 0.4 copy-done.5
  55.0 0.5 copy.15
  55.5 2.1 copy.18
  57.7 2.8 copy.11
  60.5 2.1 broadcast_in_dim.2
  62.6 4.4 %convert_element_type.81 = f32[512,896]{0,1:T(8,128)} reshape(f32[8,64,14,64]{1,0,3,2:T(8,128)} %broadcast_in_dim.2) | data formatting | bytes 3670016 | tf_op jit(solution)/shard_map/convert_element_type | solution.py:19
  67.1 3.5 fusion.3
  70.6 28.7 %all_to_all.64 = bf16[512,4,224]{0,2,1:T(8,128)(2,1)S(1)} all-to-all(bf16[512,4,224]{0,2,1:T(8,128)(2,1)S(1)} %bitcast.57), channel_id=1, replica_groups=mesh['y'=4,'x'=4,'z'=8,'core'=2] {'y'}, dimensions={1} | all-to-all | bytes 1835008 | tf_op jit(solution)/shard_map/all_to_all | solution.py:44
  99.3 0.1 copy.24
  99.4 103.5 %all-gather.5.cloned.1.call-done = bf16[3584,2048]{1,0:T(8,128)(2,1)} async-done(((bf16[3584,512]{1,0:T(8,128)(2,1)}), bf16[3584,2048]{1,0:T(8,128)(2,1)}) %all-gather.5.cloned.1.call-update) | async-done | bytes 14680080 | tf_op jit(solution)/shard_map/all_gather | solution.py:30
  202.9 10.8 %fusion = bf16[3584,224]{0,1:T(8,128)(2,1)} fusion(bf16[2048,224]{0,1:T(8,128)(2,1)S(1)} %bitcast.58, bf16[3584,2048]{1,0:T(8,128)(2,1)} %all-gather.5.cloned.1.call-done), kind=kOutput, calls=%fused_computation.2 | convolution fusion | flops 3289137152 | bytes 17203200 | tf_op jit(solution)/shard_map/dot_general | solution.py:45
  213.7 0.0 all-reduce.5.cloned.1.call-start
  213.8 56.0 %all-reduce.3.cloned.1.call-done = bf16[3584,224]{0,1:T(8,128)(2,1)} async-done(((bf16[3584,224]{0,1:T(8,128)(2,1)}), bf16[3584,224]{0,1:T(8,128)(2,1)}) %all-reduce.3.cloned.1.call-update) | async-done | bytes 1605648 | tf_op jit(solution)/shard_map/psum | solution.py:46
  269.8 9.2 %convolution_convert_fusion.3 = bf16[224,2048]{1,0:T(8,128)(2,1)S(1)} fusion(bf16[3584,2048]{1,0:T(8,128)(2,1)} %all-gather.5.cloned.1.call-done, bf16[3584,224]{0,1:T(8,128)(2,1)} %all-reduce.3.cloned.1.call-done), kind=kOutput, calls=%fused_computation.9 | convolution fusion | flops 3291201536 | bytes 17203200 | tf_op jit(solution)/shard_map/dot_general | solution.py:23
  279.1 0.1 copy.29
  279.1 17.6 %all_to_all.65 = bf16[4,512,224]{1,2,0:T(8,128)(2,1)S(1)} all-to-all(bf16[4,512,224]{1,2,0:T(8,128)(2,1)S(1)} %bitcast.54), channel_id=1, replica_groups=mesh['y'=4,'x'=4,'z'=8,'core'=2] {'y'}, dimensions={0} | all-to-all | bytes 1835008 | tf_op jit(solution)/shard_map/all_to_all | solution.py:49
  296.8 2.6 fusion.5
  299.4 14.5 %all_to_all.66 = bf16[512,4,224]{0,2,1:T(8,128)(2,1)S(1)} all-to-all(bf16[512,4,224]{0,2,1:T(8,128)(2,1)S(1)} %bitcast.52), channel_id=1, replica_groups=mesh['y'=4,'x'=4,'z'=8,'core'=2] {'y'}, dimensions={1} | all-to-all | bytes 1835008 | tf_op jit(solution)/shard_map/all_to_all | solution.py:44
  313.9 0.1 copy.25
  314.0 10.8 %fusion.1 = bf16[3584,224]{0,1:T(8,128)(2,1)} fusion(bf16[2048,224]{0,1:T(8,128)(2,1)S(1)} %bitcast.61, bf16[3584,2048]{1,0:T(8,128)(2,1)} %all-gather.5.cloned.1.call-done), kind=kOutput, calls=%fused_computation.3 | convolution fusion | flops 3289137152 | bytes 17203200 | tf_op jit(solution)/shard_map/dot_general | solution.py:45
  324.9 54.1 %all-reduce.5.cloned.1.call-done = bf16[3584,224]{0,1:T(8,128)(2,1)} async-done(((bf16[3584,224]{0,1:T(8,128)(2,1)}), bf16[3584,224]{0,1:T(8,128)(2,1)}) %all-reduce.5.cloned.1.call-update) | async-done | bytes 1605648 | tf_op jit(solution)/shard_map/psum | solution.py:46
  379.0 9.1 %convolution_convert_fusion.2 = bf16[224,2048]{1,0:T(8,128)(2,1)S(1)} fusion(bf16[3584,2048]{1,0:T(8,128)(2,1)} %all-gather.5.cloned.1.call-done, bf16[3584,224]{0,1:T(8,128)(2,1)} %all-reduce.5.cloned.1.call-done), kind=kOutput, calls=%fused_computation.8 | convolution fusion | flops 3291201536 | bytes 17203200 | tf_op jit(solution)/shard_map/dot_general | solution.py:23
  388.1 0.1 copy.28
  388.2 17.5 %all_to_all.67 = bf16[4,512,224]{1,2,0:T(8,128)(2,1)S(1)} all-to-all(bf16[4,512,224]{1,2,0:T(8,128)(2,1)S(1)} %bitcast.56), channel_id=1, replica_groups=mesh['y'=4,'x'=4,'z'=8,'core'=2] {'y'}, dimensions={0} | all-to-all | bytes 1835008 | tf_op jit(solution)/shard_map/all_to_all | solution.py:49
  405.7 3.8 fusion.17
  409.5 2.7 copy.21
  (23 shorter events, 0.1 us)
Async XLA Ops:
  6.5 47.2 %all-gather.3.cloned.1.call-start = ((), (), s32[]{:S(2)}) async-start(), calls=%async_computation.4 | async-start | bytes 3899392 | tf_op jit(solution)/shard_map/all_gather | solution.py:29
  7.3 195.7 %all-gather.5.cloned.1.call-start = ((), (), s32[]{:S(2)}) async-start(), calls=%async_computation.5 | async-start | bytes 18350080 | tf_op jit(solution)/shard_map/all_gather | solution.py:30
  53.8 0.7 copy-start.6
  53.8 0.7 copy-start.7
  53.8 1.2 copy-start.5
  53.8 216.0 %all-reduce.3.cloned.1.call-start = ((), (), s32[]{:S(2)}) async-start(), calls=%async_computation.6 | async-start | bytes 3211264 | tf_op jit(solution)/shard_map/psum | solution.py:46
  55.5 11.6 %copy-start.3 = (bf16[512,896]{0,1:T(8,128)(2,1)}, bf16[512,896]{0,1:T(8,128)(2,1)S(1)}, u32[]{:S(2)}) copy-start(bf16[512,896]{0,1:T(8,128)(2,1)S(1)} %copy.15) | copy-start | bytes 2752516
  62.6 4.5 %copy-start.8 = (s32[896]{0:T(1024)S(1)}, s32[896]{0:T(1024)}, u32[]{:S(2)}) copy-start(s32[896]{0:T(1024)} %param.11) | copy-start | bytes 10756
  213.7 165.2 %all-reduce.5.cloned.1.call-start = ((), (), s32[]{:S(2)}) async-start(), calls=%async_computation.7 | async-start | bytes 3211264 | tf_op jit(solution)/shard_map/psum | solution.py:46
  269.8 27.0 %copy-start.4 = (bf16[512,896]{0,1:T(8,128)(2,1)S(1)}, bf16[512,896]{0,1:T(8,128)(2,1)}, u32[]{:S(2)}) copy-start(bf16[512,896]{0,1:T(8,128)(2,1)} %copy-done.3) | copy-start | bytes 2752516
  279.0 17.8 %copy-start = (f32[512,896]{0,1:T(8,128)S(1)}, f32[512,896]{0,1:T(8,128)}, u32[]{:S(2)}) copy-start(f32[512,896]{0,1:T(8,128)} %convert_element_type.81) | copy-start | bytes 5505028
  279.1 17.7 %copy-start.2 = (s32[512,896]{0,1:T(8,128)S(1)}, s32[512,896]{0,1:T(8,128)}, u32[]{:S(2)}) copy-start(s32[512,896]{0,1:T(8,128)} %copy.11) | copy-start | bytes 5505028
  388.1 17.6 %copy-start.1 = (f32[512,896]{0,1:T(8,128)S(1)}, f32[512,896]{0,1:T(8,128)}, u32[]{:S(2)}) copy-start(f32[512,896]{0,1:T(8,128)} %convert_element_type.81) | copy-start | bytes 5505028
Sparse Core Ops, SparseCore 0:
  9.2 44.5 all-gather.2
  55.6 147.3 all-gather.4
  213.9 55.9 all-reduce.2
  325.0 53.9 all-reduce.4

commit v2 on v1

v2 whole, which is shorter than its diff:
```python
import functools

import jax
import jax.numpy as jnp
from jax import lax
from jax.experimental import pallas as pl
from jax.experimental.pallas import tpu as pltpu
from jax.sharding import Mesh
from jax.sharding import PartitionSpec as P

BLOCK = 64
ITERS = 2
step_rate = 20.0
reg_weight = 0.05
base_scale = 0.02

NY, NX, NZ = 4, 4, 8
SIZES = {"y": NY, "x": NX, "z": NZ, "core": 2}
TOK = 3584
SH = 224
HALF = 112
CH = 448
FEAT = 512
COLS = 896
TILE = 224
UNIT = 32
F32, BF16 = jnp.float32, jnp.bfloat16


def neighbour(axis, offset):
    size = SIZES[axis]
    return {axis: lax.rem(lax.axis_index(axis) + offset + size, size)}


def remote(src, dst, send_sem, recv_sem, axis, offset):
    return pltpu.make_async_remote_copy(
        src_ref=src,
        dst_ref=dst,
        send_sem=send_sem,
        recv_sem=recv_sem,
        device_id=neighbour(axis, offset),
        device_id_type=pl.DeviceIdType.MESH,
    )


def kernel(
    tok_ref, w_ref, v_ref, fc_ref, sc_ref, zp_ref, kept_ref, out_ref,
    x_buf, vt, ft, tt, sct, zpt, w_out, w_all, r_out, r_in, s_all, g_acc, g_out, g_all,
    ya_s, ya_r, za_s, za_r, zb_s, zb_r, yb_s, yb_r, da_s, da_r, db_s, db_r,
    ws_s, ws_r, rs_s, rs_r, ag_s, ag_r, gs_s, gs_r,
):
    y, x, z, core = (lax.axis_index(name) for name in ("y", "x", "z", "core"))

    barrier = pltpu.get_barrier_semaphore()
    partners = [("y", d) for d in (1, 2, 3)] + [("x", d) for d in (1, 2, 3)]
    partners += [("z", 1), ("z", -1), ("core", 1)]
    for axis, offset in partners:
        pl.semaphore_signal(
            barrier, 1, device_id=neighbour(axis, offset), device_id_type=pl.DeviceIdType.MESH
        )
    pl.semaphore_wait(barrier, len(partners))

    def place(j):
        off = ((j + 1) // 2) * (1 - 2 * lax.rem(j, 2))
        return lax.rem(z + off + NZ, NZ)

    def part(zz, cc, b, first=0, rows=HALF):
        return pl.ds(pl.multiple_of((zz * 2 + cc) * SH + b * HALF + first, 16), rows)

    def y_a(d):
        ref = x_buf.at[y, part(z, core, 0)]
        return remote(ref, ref, ya_s.at[d - 1], ya_r.at[d - 1], "y", d)

    def z_a(j, direction):
        ref = x_buf.at[:, part(place_sent(j, direction), core, 0)]
        return remote(ref, ref, za_s.at[j], za_r.at[j], "z", direction)

    def z_a_last(h, direction):
        ref = x_buf.at[pl.ds(2 * h, 2), part(place_sent(NZ - 1, direction), core, 0)]
        return remote(ref, ref, za_s.at[NZ - 1 + h], za_r.at[NZ - 1 + h], "z", direction)

    def z_b(j, direction):
        ref = x_buf.at[y, part(place_sent(j, direction), core, 1)]
        return remote(ref, ref, zb_s.at[j], zb_r.at[j], "z", direction)

    def z_b_last(h, direction):
        ref = x_buf.at[y, part(place_sent(NZ - 1, direction), core, 1, 64 * h, (64, 48)[h])]
        return remote(ref, ref, zb_s.at[NZ - 1 + h], zb_r.at[NZ - 1 + h], "z", direction)

    def place_sent(j, direction):
        return lax.rem(z - direction * ((j + 1) // 2 - 1) + NZ, NZ)

    def y_b(j, d):
        ref = x_buf.at[y, part(place(j), core, 1)]
        return remote(ref, ref, yb_s.at[j, d - 1], yb_r.at[j, d - 1], "y", d)

    def sib(j, b, sems):
        ref = x_buf.at[:, part(place(j), core, b)]
        return remote(ref, ref, sems[0].at[j], sems[1].at[j], "core", 1)

    def rs(j, d):
        q = lax.rem(x + d, NX)
        src = r_out.at[j, pl.ds(pl.multiple_of(q * HALF, 16), HALF)]
        return remote(src, r_in.at[j, d - 1], rs_s.at[j, d - 1], rs_r.at[j, d - 1], "x", d)

    def ag(j, d):
        ref = s_all.at[j, pl.ds(pl.multiple_of(x * HALF, 16), HALF)]
        return remote(ref, ref, ag_s.at[j, d - 1], ag_r.at[j, d - 1], "x", d)

    def w_copy(it, d):
        b = lax.rem(y + d, NY)
        return remote(w_out.at[b], w_all.at[y], ws_s.at[it, d - 1], ws_r.at[it, d - 1], "y", d)

    def g_copy(it, d):
        b = lax.rem(y + d, NY)
        return remote(g_out.at[b], g_all.at[y], gs_s.at[it, d - 1], gs_r.at[it, d - 1], "y", d)

    x_buf[y, pl.ds(pl.multiple_of((z * 2 + core) * SH, SH), SH), :] = tok_ref[...]
    for d in (2, 1, 3):
        y_a(d).start()
    z_b(1, 1).start()
    z_b(2, -1).start()
    for d in (2, 1, 3):
        y_b(0, d).start()

    def turn(ct, carry):
        c0 = pl.multiple_of(ct * 128, 128)
        cols = pl.ds(c0, 128)
        scale = base_scale * jnp.exp2(sc_ref[:, cols].astype(F32) * 0.25)
        sct[cols, :] = jnp.broadcast_to(scale, (128, 128)).T
        zpt[cols, :] = jnp.broadcast_to(zp_ref[:, cols].astype(F32), (128, 128)).T
        for rt in range(FEAT // 128):
            rows = slice(rt * 128, rt * 128 + 128)
            vt[cols, rows] = v_ref[rows, cols].T
            ft[cols, rows] = fc_ref[rows, cols].astype(F32).T
            tt[cols, rows] = w_ref[rows, cols].astype(F32).T.astype(BF16)
        return carry

    lax.fori_loop(0, COLS // 128, turn, 0)

    def gather_step(j):
        @pl.when(j == 0)
        def _():
            for d in (1, 2, 3):
                y_a(d).wait_recv()
            z_a(1, 1).start()
            z_a(2, -1).start()

        direction = 2 * lax.rem(j, 2) - 1

        @pl.when((j > 0) & (j < NZ - 1))
        def _():
            z_b(j, direction).wait_recv()

        @pl.when((j > 0) & (j < NZ - 3))
        def _():
            z_b(j + 2, direction).start()

        @pl.when(j == NZ - 3)
        def _():
            z_b_last(0, 1).start()

        @pl.when(j == NZ - 2)
        def _():
            z_b_last(1, -1).start()

        @pl.when(j == NZ - 1)
        def _():
            z_b_last(0, 1).wait_recv()
            z_b_last(1, -1).wait_recv()

        @pl.when(j > 0)
        def _():
            for d in (2, 1, 3):
                y_b(j, d).start()

        @pl.when((j > 0) & (j < NZ - 1))
        def _():
            z_a(j, direction).wait_recv()

        @pl.when((j > 0) & (j < NZ - 3))
        def _():
            z_a(j + 2, direction).start()

        @pl.when(j == NZ - 3)
        def _():
            z_a_last(0, 1).start()

        @pl.when(j == NZ - 2)
        def _():
            z_a_last(1, -1).start()

        @pl.when(j == NZ - 1)
        def _():
            z_a_last(0, 1).wait_recv()
            z_a_last(1, -1).wait_recv()

        sib(j, 0, (da_s, da_r)).start()

    def sibling_step(j):
        for d in (1, 2, 3):
            y_b(j, d).wait_recv()
        sib(j, 1, (db_s, db_r)).start()

    def partial_step(j):
        rows = pl.ds(pl.multiple_of(place(j) * CH, CH), CH)
        acc = None
        for g in range(NY):
            term = lax.dot_general(
                x_buf[g, rows, :], w_all[g], (((1,), (1,)), ((), ())), preferred_element_type=F32
            )
            acc = term if acc is None else acc + term
        r_out[j] = acc.astype(BF16)
        for d in (2, 1, 3):
            rs(j, d).start()

    def sum_step(j):
        mine = pl.ds(pl.multiple_of(x * HALF, 16), HALF)
        total = r_out[j, mine, :].astype(F32)
        for d in (1, 2, 3):
            rs(j, d).wait_recv()
            total = total + r_in[j, d - 1].astype(F32)
        s_all[j, mine, :] = ((2.0 / TOK) * total).astype(BF16)
        for d in (2, 1, 3):
            ag(j, d).start()

    def gradient_step(j):
        for d in (1, 2, 3):
            ag(j, d).wait_recv()
            rs(j, d).wait_send()
            ag(j, d).wait_send()

        @pl.when(j == 0)
        def _():
            g_acc[...] = jnp.zeros_like(g_acc)

        rows = pl.ds(pl.multiple_of(place(j) * CH, CH), CH)
        turned = s_all[j].astype(F32).T.astype(BF16)
        for g in range(NY):
            g_acc[g] += jnp.dot(turned, x_buf[g, rows, :], preferred_element_type=F32)

    def columns(u, b):
        r0 = pl.multiple_of(b * TILE + u * UNIT, UNIT)
        rows = pl.ds(r0, UNIT)
        kept = jnp.concatenate([kept_ref[r0 // BLOCK]] * (UNIT // 8), axis=0)
        wide = lambda ref: jnp.concatenate([ref[rows, :]] * (FEAT // 128), axis=1)
        return rows, kept, wide(sct), wide(zpt)

    def delta(v, f, t, kept, scale, zero):
        levels = jnp.clip(f + jax.nn.sigmoid(v), 0.0, 15.0)
        return (kept * (scale * (levels - zero) - t)).astype(BF16)

    def first_delta(b, dst):
        def unit(u, carry):
            rows, kept, scale, zero = columns(u, b)
            here = pl.ds(pl.multiple_of(u * UNIT, UNIT), UNIT)
            dst[here, :] = delta(
                vt[rows, :], ft[rows, :], tt[rows, :].astype(F32), kept, scale, zero
            )
            return carry

        lax.fori_loop(0, TILE // UNIT, unit, 0)

    def update(b, dst):
        def unit(u, carry):
            rows, kept, scale, zero = columns(u, b)
            here = pl.ds(pl.multiple_of(u * UNIT, UNIT), UNIT)
            v, f = vt[rows, :], ft[rows, :]
            relaxed = jax.nn.sigmoid(v)
            in_range = ((f >= 0.0) & (f <= 14.0)).astype(F32)
            centered = 2.0 * relaxed - 1.0
            gradient = g_all[b, here, :].astype(F32)
            descent = gradient * scale * in_range - reg_weight * 8.0 * (
                centered * centered * centered
            )
            v = v - step_rate * kept * descent * relaxed * (1.0 - relaxed)
            vt[rows, :] = v
            if dst is not None:
                dst[here, :] = delta(v, f, tt[rows, :].astype(F32), kept, scale, zero)
            return carry

        lax.fori_loop(0, TILE // UNIT, unit, 0)

    def send_gradient(it):
        for d in (2, 1, 3):
            b = lax.rem(y + d, NY)
            g_out[b] = g_acc[b].astype(BF16)
            g_copy(it, d).start()
        g_all[y] = g_acc[y].astype(BF16)

    gather_step(0)
    for d in (2, 1, 3):
        b = lax.rem(y + d, NY)
        first_delta(b, w_out.at[b])
        w_copy(0, d).start()
    first_delta(y, w_all.at[y])

    def stage(s, carry):
        pl.when(s < NZ)(lambda: gather_step(s))
        pl.when((s >= 1) & (s < NZ + 1))(lambda: sibling_step(s - 1))

        @pl.when(s == 2)
        def _():
            for d in (1, 2, 3):
                w_copy(0, d).wait_recv()

        @pl.when((s >= 2) & (s < NZ + 2))
        def _():
            sib(s - 2, 0, (da_s, da_r)).wait_recv()
            sib(s - 2, 1, (db_s, db_r)).wait_recv()
            partial_step(s - 2)

        pl.when((s >= 3) & (s < NZ + 3))(lambda: sum_step(s - 3))
        pl.when(s >= 4)(lambda: gradient_step(s - 4))
        return carry

    lax.fori_loop(1, NZ + 4, stage, 0)
    send_gradient(0)
    for d in (1, 2, 3):
        w_copy(0, d).wait_send()
    update(y, w_all.at[y])
    for d in (1, 3, 2):
        g_copy(0, d).wait_recv()
        b = lax.rem(y - d + NY, NY)
        update(b, w_out.at[b])
        w_copy(1, NY - d).start()

    for d in (1, 2, 3):
        w_copy(1, d).wait_recv()

    def stage_two(s, carry):
        pl.when(s < NZ)(lambda: partial_step(s))
        pl.when((s >= 1) & (s < NZ + 1))(lambda: sum_step(s - 1))
        pl.when(s >= 3)(lambda: gradient_step(s - 3))
        return carry

    lax.fori_loop(0, NZ + 3, stage_two, 0)
    for d in (1, 2, 3):
        g_copy(0, d).wait_send()
    send_gradient(1)
    update(y, None)
    for d in (1, 3, 2):
        g_copy(1, d).wait_recv()
        update(lax.rem(y - d + NY, NY), None)

    def turn_back(ct, carry):
        cols = pl.ds(pl.multiple_of(ct * 128, 128), 128)
        for rt in range(FEAT // 128):
            rows = slice(rt * 128, rt * 128 + 128)
            out_ref[rows, cols] = vt[cols, rows].T
        return carry

    lax.fori_loop(0, COLS // 128, turn_back, 0)

    for d in (1, 2, 3):
        y_a(d).wait_send()
        w_copy(1, d).wait_send()
        g_copy(1, d).wait_send()
    for j in range(1, NZ - 1):
        z_a(j, 2 * (j % 2) - 1).wait_send()
        z_b(j, 2 * (j % 2) - 1).wait_send()
    for h in range(2):
        z_a_last(h, 1 - 2 * h).wait_send()
        z_b_last(h, 1 - 2 * h).wait_send()

    def drain(j, carry):
        for d in (1, 2, 3):
            y_b(j, d).wait_send()
        sib(j, 0, (da_s, da_r)).wait_send()
        sib(j, 1, (db_s, db_r)).wait_send()
        return carry

    lax.fori_loop(0, NZ, drain, 0)


def per_device(tokens, weight, rounding, floor_codes, scale_codes, zero_codes, block_mask):
    kept = jnp.broadcast_to(
        block_mask.T.astype(F32)[:, None, :, None], (COLS // BLOCK, 8, FEAT // BLOCK, BLOCK)
    ).reshape(COLS // BLOCK, 8, FEAT)
    dma = lambda *shape: pltpu.SemaphoreType.DMA(shape)
    pair = lambda *shape: [dma(*shape), dma(*shape)]
    vmem = pl.BlockSpec(memory_space=pltpu.VMEM)
    return pl.pallas_call(
        kernel,
        out_shape=jax.ShapeDtypeStruct((FEAT, COLS), F32),
        in_specs=[vmem] * 7,
        out_specs=vmem,
        scratch_shapes=[
            pltpu.VMEM((NY, TOK, FEAT), BF16),
            pltpu.VMEM((COLS, FEAT), F32),
            pltpu.VMEM((COLS, FEAT), F32),
            pltpu.VMEM((COLS, FEAT), BF16),
            pltpu.VMEM((COLS, 128), F32),
            pltpu.VMEM((COLS, 128), F32),
            pltpu.VMEM((NY, TILE, FEAT), BF16),
            pltpu.VMEM((NY, TILE, FEAT), BF16),
            pltpu.VMEM((NZ, CH, TILE), BF16),
            pltpu.VMEM((NZ, NX - 1, HALF, TILE), BF16),
            pltpu.VMEM((NZ, CH, TILE), BF16),
            pltpu.VMEM((NY, TILE, FEAT), F32),
            pltpu.VMEM((NY, TILE, FEAT), BF16),
            pltpu.VMEM((NY, TILE, FEAT), BF16),
            *pair(3), *pair(NZ + 1), *pair(NZ + 1), *pair(NZ, 3), *pair(NZ), *pair(NZ),
            *pair(ITERS, 3), *pair(NZ, 3), *pair(NZ, 3), *pair(ITERS, 3),
        ],
        compiler_params=pltpu.CompilerParams(
            collective_id=0, has_side_effects=True, vmem_limit_bytes=60 << 20
        ),
        cost_estimate=pl.CostEstimate(
            flops=4 * 2 * TOK * FEAT * COLS, bytes_accessed=8 << 20, transcendentals=4 * FEAT * COLS
        ),
        name="adaround",
    )(
        tokens, weight, rounding, floor_codes,
        scale_codes.reshape(1, COLS), zero_codes.reshape(1, COLS), kept,
    )


def solution(mesh):
    fine = Mesh(mesh.devices.reshape(NY, NX, NZ, 2), ("y", "x", "z", "core"))
    loop, dp = ("y", "x"), ("z", "core")
    placed = (
        P(dp, loop),
        P(loop, dp),
        P(loop, dp),
        P(loop, dp),
        P(dp),
        P(dp),
        P(loop, dp),
    )
    return jax.shard_map(
        per_device, mesh=fine, in_specs=placed, out_specs=P(loop, dp), check_vma=False
    )
```

time: 420 us -> 173 us (0.41)
  waiting for transfers between devices: 261 us -> 0 us
  Pallas kernels: 0 us -> 165 us
  blocking collectives: 78.3 us -> 0 us
  matrix products: 40 us -> 0 us
  between operations: 13.3 us -> 0.01 us
  local copies, waits for them, and re-layouts: 16.3 us -> 6.36 us
  other arithmetic: 9.91 us -> 0.69 us
    pallas_call x0 -> x1, Pallas kernels: none -> 165 us  [per_device(): pl.pallas_call(kernel, out_shape=jax.ShapeDtypeStruct((FEAT, COLS), F32),...]
    all_gather x2 -> x0, waiting for transfers between devices: 150 us -> none  [the longest x1 104 us: per_device(): gathered = lax.all_gather(gathered, 'y', axis=1, tiled=True)]
    psum x2 -> x0, waiting for transfers between devices: 110 us -> none  [per_device(): lax.psum(partial_sum.astype(jnp.bfloat16), 'x').astype(jnp.float32)]
    all_to_all x4 -> x0, blocking collectives: 78.3 us -> none  [the longest x2 43.2 us: per_device(): lax.all_to_all(w_delta, 'y', split_axis=1, concat_axis=0, tiled=True)]
    dot_general x4 -> x0, matrix products: 40 us -> none  [the longest x2 21.6 us: per_device(): partial_sum = jnp.dot(gathered, w_tall, preferred_element_type=jnp.float32)]
    convert_element_type x4 -> x1, other arithmetic: 6.1 us -> 0.69 us  [per_device(): block_mask.T.astype(F32)[:, None, :, None]]
    convert_element_type x2 -> x1, local copies, waits for them, and re-layouts: 4.53 us -> 0.09 us  [per_device(): block_mask.T.astype(F32)[:, None, :, None]]
  transfers between devices with their start and end apart: 4 -> 0, of which waited for: 4 -> 0; matrix products, arithmetic and copies ran while one was open for 4% -> 0% of each run, Pallas kernels for 0% -> 0%
where the time goes in v2:
time: 173 us; the launch traced here: 172 us
  Pallas kernels  165 us (95%)
  local copies, waits for them, and re-layouts  6.36 us (4%)
    pallas_call x1, Pallas kernels, per_device(): pl.pallas_call(kernel, out_shape=jax.ShapeDtypeStruct((FEAT, COLS), F32),...  165 us

profile of v2, /device:TPU:2, one launch (start us, length us, event | category | flops | bytes accessed | tf_op | source)
XLA Modules:
  0.0 172.4 jit_solution(7022823752945206033)
XLA Ops:
  0.0 1.3 reshape.9.sc_ref
  1.3 1.3 reshape.10.zp_ref
  2.6 0.7 convert_bitcast_fusion
  3.2 0.1 copy.8
  3.3 0.1 broadcast_in_dim.10
  3.4 0.1 broadcast_in_dim.11
  3.5 0.7 broadcast_in_dim.12.kept_ref
  4.2 165.3 %adaround.1 = f32[512,896]{1,0:T(8,128)} custom-call(bf16[224,512]{1,0:T(8,128)(2,1)} %tok_ref.1, bf16[512,896]{1,0:T(8,128)(2,1)} %w_ref.1, f32[512,896]{1,0:T(8,128)} %v_ref.1, s32[512,896]{1,0:T(8,128)} %fc_ref.1, s32[1,896]{1,0:T(1,128)} %reshape.9.sc_ref, s32[1,896]{1,0:T(1,128)} %reshape.10.zp_ref, f32[14,8,512]{2,1,0:T(8,128)} %broadcast_in_dim.12.kept_ref), custom_call_target="tpu_custom_call" | custom-call | flops 13153337344 | bytes 8388608 | tf_op jit(solution)/shard_map/adaround/pallas_call | solution.py:383
  169.6 2.8 %copy.10 = f32[512,896]{1,0:T(8,128)} copy(f32[512,896]{1,0:T(8,128)} %adaround.1) | data formatting | bytes 3670016

commit v3 on v2

--- a/solution.py
+++ b/solution.py
@@ -23,7 +23,8 @@
 FEAT = 512
 COLS = 896
 TILE = 224
-UNIT = 32
+HC = 112
+UNIT = 16
 F32, BF16 = jnp.float32, jnp.bfloat16
 
 
@@ -44,12 +45,21 @@
 
 
 def kernel(
-    tok_ref, w_ref, v_ref, fc_ref, sc_ref, zp_ref, kept_ref, out_ref,
-    x_buf, vt, ft, tt, sct, zpt, w_out, w_all, r_out, r_in, s_all, g_acc, g_out, g_all,
+    tok_ref, w_hbm, v_hbm, fc_hbm, sc_ref, zp_ref, mask_ref, out_ref,
+    w_ref, v_ref, fc_ref,
+    x_buf, vt, ft, tt, sct, zpt, kept_ref, w_out, w_all, r_out, r_in, s_all, g_acc, g_out, g_all,
+    r2_out, r2_in, s2_all, in_sem,
     ya_s, ya_r, za_s, za_r, zb_s, zb_r, yb_s, yb_r, da_s, da_r, db_s, db_r,
-    ws_s, ws_r, rs_s, rs_r, ag_s, ag_r, gs_s, gs_r,
+    ws_s, ws_r, w2_s, w2_r, rs_s, rs_r, ag_s, ag_r, rs2_s, rs2_r, ag2_s, ag2_r, gs_s, gs_r,
 ):
     y, x, z, core = (lax.axis_index(name) for name in ("y", "x", "z", "core"))
+
+    inputs = [
+        pltpu.make_async_copy(src, dst, in_sem.at[i])
+        for i, (src, dst) in enumerate(((v_hbm, v_ref), (fc_hbm, fc_ref), (w_hbm, w_ref)))
+    ]
+    for copy in inputs:
+        copy.start()
 
     barrier = pltpu.get_barrier_semaphore()
     partners = [("y", d) for d in (1, 2, 3)] + [("x", d) for d in (1, 2, 3)]
@@ -71,13 +81,9 @@
         ref = x_buf.at[y, part(z, core, 0)]
         return remote(ref, ref, ya_s.at[d - 1], ya_r.at[d - 1], "y", d)
 
-    def z_a(j, direction):
-        ref = x_buf.at[:, part(place_sent(j, direction), core, 0)]
-        return remote(ref, ref, za_s.at[j], za_r.at[j], "z", direction)
-
-    def z_a_last(h, direction):
-        ref = x_buf.at[pl.ds(2 * h, 2), part(place_sent(NZ - 1, direction), core, 0)]
-        return remote(ref, ref, za_s.at[NZ - 1 + h], za_r.at[NZ - 1 + h], "z", direction)
+    def z_a(j, d, direction):
+        ref = x_buf.at[lax.rem(y - d + NY, NY), part(place_sent(j, direction), core, 0)]
+        return remote(ref, ref, za_s.at[j, d], za_r.at[j, d], "z", direction)
 
     def z_b(j, direction):
         ref = x_buf.at[y, part(place_sent(j, direction), core, 1)]
@@ -107,19 +113,39 @@
         ref = s_all.at[j, pl.ds(pl.multiple_of(x * HALF, 16), HALF)]
         return remote(ref, ref, ag_s.at[j, d - 1], ag_r.at[j, d - 1], "x", d)
 
-    def w_copy(it, d):
+    def half(h, first=0):
+        return pl.ds(pl.multiple_of(first + h * HC, 16), HC)
+
+    def w_copy(d):
         b = lax.rem(y + d, NY)
-        return remote(w_out.at[b], w_all.at[y], ws_s.at[it, d - 1], ws_r.at[it, d - 1], "y", d)
-
-    def g_copy(it, d):
+        return remote(w_out.at[b], w_all.at[y], ws_s.at[d - 1], ws_r.at[d - 1], "y", d)
+
+    def w2_copy(h, d):
         b = lax.rem(y + d, NY)
-        return remote(g_out.at[b], g_all.at[y], gs_s.at[it, d - 1], gs_r.at[it, d - 1], "y", d)
+        src, dst = w_out.at[b, half(h)], w_all.at[y, half(h)]
+        return remote(src, dst, w2_s.at[h, d - 1], w2_r.at[h, d - 1], "y", d)
+
+    def g_copy(it, h, d):
+        b = lax.rem(y + d, NY)
+        src, dst = g_out.at[b, half(h)], g_all.at[y, half(h)]
+        return remote(src, dst, gs_s.at[it, h, d - 1], gs_r.at[it, h, d - 1], "y", d)
+
+    def rs2(u, d):
+        q = lax.rem(x + d, NX)
+        src = r2_out.at[u, pl.ds(pl.multiple_of(q * HALF, 16), HALF)]
+        return remote(src, r2_in.at[u, d - 1], rs2_s.at[u, d - 1], rs2_r.at[u, d - 1], "x", d)
+
+    def ag2(u, d):
+        ref = s2_all.at[u, pl.ds(pl.multiple_of(x * HALF, 16), HALF)]
+        return remote(ref, ref, ag2_s.at[u, d - 1], ag2_r.at[u, d - 1], "x", d)
 
     x_buf[y, pl.ds(pl.multiple_of((z * 2 + core) * SH, SH), SH), :] = tok_ref[...]
     for d in (2, 1, 3):
         y_a(d).start()
     z_b(1, 1).start()
     z_b(2, -1).start()
+    z_a(1, 0, 1).start()
+    z_a(2, 0, -1).start()
     for d in (2, 1, 3):
         y_b(0, d).start()
 
@@ -136,66 +162,52 @@
             tt[cols, rows] = w_ref[rows, cols].astype(F32).T.astype(BF16)
         return carry
 
+    spread = (
+        lax.broadcasted_iota(jnp.int32, (8, FEAT), 1) // BLOCK
+        == lax.broadcasted_iota(jnp.int32, (8, FEAT), 0)
+    ).astype(F32)
+    kept_ref[...] = jnp.dot(
+        mask_ref[...].astype(F32).T.astype(BF16), spread.astype(BF16), preferred_element_type=F32
+    )
+    for copy in inputs:
+        copy.wait()
     lax.fori_loop(0, COLS // 128, turn, 0)
 
-    def gather_step(j):
-        @pl.when(j == 0)
-        def _():
-            for d in (1, 2, 3):
-                y_a(d).wait_recv()
-            z_a(1, 1).start()
-            z_a(2, -1).start()
-
-        direction = 2 * lax.rem(j, 2) - 1
-
-        @pl.when((j > 0) & (j < NZ - 1))
-        def _():
-            z_b(j, direction).wait_recv()
-
-        @pl.when((j > 0) & (j < NZ - 3))
-        def _():
-            z_b(j + 2, direction).start()
-
-        @pl.when(j == NZ - 3)
-        def _():
-            z_b_last(0, 1).start()
-
-        @pl.when(j == NZ - 2)
-        def _():
-            z_b_last(1, -1).start()
-
-        @pl.when(j == NZ - 1)
-        def _():
+    last = NZ - 1
+
+    def way(j):
+        return 1 if j % 2 else -1
+
+    def gather_b(j):
+        if j == last:
             z_b_last(0, 1).wait_recv()
             z_b_last(1, -1).wait_recv()
-
-        @pl.when(j > 0)
-        def _():
-            for d in (2, 1, 3):
-                y_b(j, d).start()
-
-        @pl.when((j > 0) & (j < NZ - 1))
-        def _():
-            z_a(j, direction).wait_recv()
-
-        @pl.when((j > 0) & (j < NZ - 3))
-        def _():
-            z_a(j + 2, direction).start()
-
-        @pl.when(j == NZ - 3)
-        def _():
-            z_a_last(0, 1).start()
-
-        @pl.when(j == NZ - 2)
-        def _():
-            z_a_last(1, -1).start()
-
-        @pl.when(j == NZ - 1)
-        def _():
-            z_a_last(0, 1).wait_recv()
-            z_a_last(1, -1).wait_recv()
-
-        sib(j, 0, (da_s, da_r)).start()
+        else:
+            z_b(j, way(j)).wait_recv()
+            if j + 2 < last:
+                z_b(j + 2, way(j)).start()
+            else:
+                z_b_last(0 if way(j) > 0 else 1, way(j)).start()
+        for d in (2, 1, 3):
+            y_b(j, d).start()
+
+    def last_way(d):
+        return 1 if d < 2 else -1
+
+    def gather_a(j, d):
+        if j == 0:
+            if d:
+                y_a(d).wait_recv()
+                z_a(1, d, 1).start()
+                z_a(2, d, -1).start()
+        elif j == last:
+            z_a(j, d, last_way(d)).wait_recv()
+        else:
+            z_a(j, d, way(j)).wait_recv()
+            if j + 2 < last:
+                z_a(j + 2, d, way(j)).start()
+            elif way(j) == last_way(d):
+                z_a(last, d, way(j)).start()
 
     def sibling_step(j):
         for d in (1, 2, 3):
@@ -239,10 +251,51 @@
         for g in range(NY):
             g_acc[g] += jnp.dot(turned, x_buf[g, rows, :], preferred_element_type=F32)
 
-    def columns(u, b):
-        r0 = pl.multiple_of(b * TILE + u * UNIT, UNIT)
+    def partial_two(u):
+        h, j = u // NZ, lax.rem(u, NZ)
+        rows = pl.ds(pl.multiple_of(place(j) * CH, CH), CH)
+        acc = None
+        for g in range(NY):
+            term = lax.dot_general(
+                x_buf[g, rows, :], w_all[g, half(h), :], (((1,), (1,)), ((), ())),
+                preferred_element_type=F32,
+            )
+            acc = term if acc is None else acc + term
+        r2_out[u] = acc.astype(BF16)
+        for d in (2, 1, 3):
+            rs2(u, d).start()
+
+    def sum_two(u):
+        mine = pl.ds(pl.multiple_of(x * HALF, 16), HALF)
+        total = r2_out[u, mine, :].astype(F32)
+        for d in (1, 2, 3):
+            rs2(u, d).wait_recv()
+            total = total + r2_in[u, d - 1].astype(F32)
+        s2_all[u, mine, :] = ((2.0 / TOK) * total).astype(BF16)
+        for d in (2, 1, 3):
+            ag2(u, d).start()
+
+    def gradient_two(u):
+        h, j = u // NZ, lax.rem(u, NZ)
+        for d in (1, 2, 3):
+            ag2(u, d).wait_recv()
+            rs2(u, d).wait_send()
+            ag2(u, d).wait_send()
+
+        @pl.when(j == 0)
+        def _():
+            g_acc[:, half(h), :] = jnp.zeros((NY, HC, FEAT), F32)
+
+        rows = pl.ds(pl.multiple_of(place(j) * CH, CH), CH)
+        turned = s2_all[u].astype(F32).T.astype(BF16)
+        for g in range(NY):
+            g_acc[g, half(h), :] += jnp.dot(
+                turned, x_buf[g, rows, :], preferred_element_type=F32
+            )
+
+    def columns(r0):
         rows = pl.ds(r0, UNIT)
-        kept = jnp.concatenate([kept_ref[r0 // BLOCK]] * (UNIT // 8), axis=0)
+        kept = jnp.broadcast_to(kept_ref[pl.ds(r0 // BLOCK, 1), :], (UNIT, FEAT))
         wide = lambda ref: jnp.concatenate([ref[rows, :]] * (FEAT // 128), axis=1)
         return rows, kept, wide(sct), wide(zpt)
 
@@ -252,8 +305,8 @@
 
     def first_delta(b, dst):
         def unit(u, carry):
-            rows, kept, scale, zero = columns(u, b)
             here = pl.ds(pl.multiple_of(u * UNIT, UNIT), UNIT)
+            rows, kept, scale, zero = columns(pl.multiple_of(b * TILE + u * UNIT, UNIT))
             dst[here, :] = delta(
                 vt[rows, :], ft[rows, :], tt[rows, :].astype(F32), kept, scale, zero
             )
@@ -261,10 +314,11 @@
 
         lax.fori_loop(0, TILE // UNIT, unit, 0)
 
-    def update(b, dst):
+    def update(b, h, dst):
         def unit(u, carry):
-            rows, kept, scale, zero = columns(u, b)
-            here = pl.ds(pl.multiple_of(u * UNIT, UNIT), UNIT)
+            u0 = pl.multiple_of(h * HC + u * UNIT, UNIT)
+            here = pl.ds(u0, UNIT)
+            rows, kept, scale, zero = columns(pl.multiple_of(b * TILE + u0, UNIT))
             v, f = vt[rows, :], ft[rows, :]
             relaxed = jax.nn.sigmoid(v)
             in_range = ((f >= 0.0) & (f <= 14.0)).astype(F32)
@@ -279,69 +333,113 @@
                 dst[here, :] = delta(v, f, tt[rows, :].astype(F32), kept, scale, zero)
             return carry
 
-        lax.fori_loop(0, TILE // UNIT, unit, 0)
-
-    def send_gradient(it):
+        lax.fori_loop(0, HC // UNIT, unit, 0)
+
+    def send_gradient(it, h):
+        rows = half(h)
         for d in (2, 1, 3):
             b = lax.rem(y + d, NY)
-            g_out[b] = g_acc[b].astype(BF16)
-            g_copy(it, d).start()
-        g_all[y] = g_acc[y].astype(BF16)
-
-    gather_step(0)
+            g_out[b, rows, :] = g_acc[b, rows, :].astype(BF16)
+            g_copy(it, h, d).start()
+        g_all[y, rows, :] = g_acc[y, rows, :].astype(BF16)
+
+    def refine_half(h):
+        update(y, h, w_all.at[y])
+        for d in (1, 3, 2):
+            g_copy(0, h, d).wait_recv()
+            b = lax.rem(y - d + NY, NY)
+            update(b, h, w_out.at[b])
+            w2_copy(h, NY - d).start()
+
+    def last_update(h):
+        update(y, h, None)
+        for d in (1, 3, 2):
+            g_copy(1, h, d).wait_recv()
+            update(lax.rem(y - d + NY, NY), h, None)
+
+    for d in range(NY):
+        gather_a(0, d)
+    sib(0, 0, (da_s, da_r)).start()
     for d in (2, 1, 3):
         b = lax.rem(y + d, NY)
         first_delta(b, w_out.at[b])
-        w_copy(0, d).start()
+        w_copy(d).start()
     first_delta(y, w_all.at[y])
 
-    def stage(s, carry):
-        pl.when(s < NZ)(lambda: gather_step(s))
-        pl.when((s >= 1) & (s < NZ + 1))(lambda: sibling_step(s - 1))
-
-        @pl.when(s == 2)
+    def arrive(j):
+        sib(j, 0, (da_s, da_r)).wait_recv()
+        sib(j, 1, (db_s, db_r)).wait_recv()
+        partial_step(j)
+
+    pairs = [(0,), (1, 2), (3, 4), (5, 6), (7,)]
+    for k in range(1, 5):
+        before, older = pairs[k - 1], pairs[k - 2] if k > 1 else ()
+        for j in pairs[k]:
+            gather_b(j)
+        for d in range(NY):
+            for j in pairs[k]:
+                gather_a(j, d)
+            if d == 0:
+                for j in before:
+                    sibling_step(j)
+                for j in older:
+                    sum_step(j)
+            if d == 1:
+                if k == 1:
+                    for e in (1, 2, 3):
+                        w_copy(e).wait_recv()
+                arrive(before[0])
+            if d == 2:
+                for j in before[1:]:
+                    arrive(j)
+            if d == 3:
+                for j in pairs[k]:
+                    sib(j, 0, (da_s, da_r)).start()
+                for j in older:
+                    gradient_step(j)
+    sibling_step(last)
+    for j in pairs[3]:
+        sum_step(j)
+    arrive(last)
+    for j in pairs[3]:
+        gradient_step(j)
+    sum_step(last)
+    gradient_step(last)
+
+    send_gradient(0, 0)
+    for d in (1, 2, 3):
+        w_copy(d).wait_send()
+    refine_half(0)
+    send_gradient(0, 1)
+    for d in (1, 2, 3):
+        w2_copy(0, d).wait_recv()
+
+    def stage_two(s, carry):
+        pl.when(s == 2)(lambda: refine_half(1))
+
+        @pl.when(s == NZ)
         def _():
             for d in (1, 2, 3):
-                w_copy(0, d).wait_recv()
-
-        @pl.when((s >= 2) & (s < NZ + 2))
+                w2_copy(1, d).wait_recv()
+
+        pl.when(s < 2 * NZ)(lambda: partial_two(s))
+        pl.when((s >= 2) & (s < 2 * NZ + 2))(lambda: sum_two(s - 2))
+        pl.when(s >= 4)(lambda: gradient_two(s - 4))
+
+        @pl.when(s == NZ + 3)
         def _():
-            sib(s - 2, 0, (da_s, da_r)).wait_recv()
-            sib(s - 2, 1, (db_s, db_r)).wait_recv()
-            partial_step(s - 2)
-
-        pl.when((s >= 3) & (s < NZ + 3))(lambda: sum_step(s - 3))
-        pl.when(s >= 4)(lambda: gradient_step(s - 4))
+            for d in (1, 2, 3):
+                g_copy(0, 0, d).wait_send()
+            send_gradient(1, 0)
+
         return carry
 
-    lax.fori_loop(1, NZ + 4, stage, 0)
-    send_gradient(0)
+    lax.fori_loop(0, 2 * NZ + 4, stage_two, 0)
     for d in (1, 2, 3):
-        w_copy(0, d).wait_send()
-    update(y, w_all.at[y])
-    for d in (1, 3, 2):
-        g_copy(0, d).wait_recv()
-        b = lax.rem(y - d + NY, NY)
-        update(b, w_out.at[b])
-        w_copy(1, NY - d).start()
-
-    for d in (1, 2, 3):
-        w_copy(1, d).wait_recv()
-
-    def stage_two(s, carry):
-        pl.when(s < NZ)(lambda: partial_step(s))
-        pl.when((s >= 1) & (s < NZ + 1))(lambda: sum_step(s - 1))
-        pl.when(s >= 3)(lambda: gradient_step(s - 3))
-        return carry
-
-    lax.fori_loop(0, NZ + 3, stage_two, 0)
-    for d in (1, 2, 3):
-        g_copy(0, d).wait_send()
-    send_gradient(1)
-    update(y, None)
-    for d in (1, 3, 2):
-        g_copy(1, d).wait_recv()
-        update(lax.rem(y - d + NY, NY), None)
+        g_copy(0, 1, d).wait_send()
+    send_gradient(1, 1)
+    last_update(0)
+    last_update(1)
 
     def turn_back(ct, carry):
         cols = pl.ds(pl.multiple_of(ct * 128, 128), 128)
@@ -354,13 +452,16 @@
 
     for d in (1, 2, 3):
         y_a(d).wait_send()
-        w_copy(1, d).wait_send()
-        g_copy(1, d).wait_send()
-    for j in range(1, NZ - 1):
-        z_a(j, 2 * (j % 2) - 1).wait_send()
-        z_b(j, 2 * (j % 2) - 1).wait_send()
+        for h in range(2):
+            w2_copy(h, d).wait_send()
+            g_copy(1, h, d).wait_send()
+    for j in range(1, last):
+        z_b(j, way(j)).wait_send()
+        for d in range(NY):
+            z_a(j, d, way(j)).wait_send()
+    for d in range(NY):
+        z_a(last, d, last_way(d)).wait_send()
     for h in range(2):
-        z_a_last(h, 1 - 2 * h).wait_send()
         z_b_last(h, 1 - 2 * h).wait_send()
 
     def drain(j, carry):
@@ -374,24 +475,25 @@
 
 
 def per_device(tokens, weight, rounding, floor_codes, scale_codes, zero_codes, block_mask):
-    kept = jnp.broadcast_to(
-        block_mask.T.astype(F32)[:, None, :, None], (COLS // BLOCK, 8, FEAT // BLOCK, BLOCK)
-    ).reshape(COLS // BLOCK, 8, FEAT)
     dma = lambda *shape: pltpu.SemaphoreType.DMA(shape)
     pair = lambda *shape: [dma(*shape), dma(*shape)]
     vmem = pl.BlockSpec(memory_space=pltpu.VMEM)
     return pl.pallas_call(
         kernel,
         out_shape=jax.ShapeDtypeStruct((FEAT, COLS), F32),
-        in_specs=[vmem] * 7,
+        in_specs=[vmem] + [pl.BlockSpec(memory_space=pl.ANY)] * 3 + [vmem] * 3,
         out_specs=vmem,
         scratch_shapes=[
+            pltpu.VMEM((FEAT, COLS), BF16),
+            pltpu.VMEM((FEAT, COLS), F32),
+            pltpu.VMEM((FEAT, COLS), jnp.int32),
             pltpu.VMEM((NY, TOK, FEAT), BF16),
             pltpu.VMEM((COLS, FEAT), F32),
             pltpu.VMEM((COLS, FEAT), F32),
             pltpu.VMEM((COLS, FEAT), BF16),
             pltpu.VMEM((COLS, 128), F32),
             pltpu.VMEM((COLS, 128), F32),
+            pltpu.VMEM((COLS // BLOCK, FEAT), F32),
             pltpu.VMEM((NY, TILE, FEAT), BF16),
             pltpu.VMEM((NY, TILE, FEAT), BF16),
             pltpu.VMEM((NZ, CH, TILE), BF16),
@@ -400,8 +502,13 @@
             pltpu.VMEM((NY, TILE, FEAT), F32),
             pltpu.VMEM((NY, TILE, FEAT), BF16),
             pltpu.VMEM((NY, TILE, FEAT), BF16),
-            *pair(3), *pair(NZ + 1), *pair(NZ + 1), *pair(NZ, 3), *pair(NZ), *pair(NZ),
-            *pair(ITERS, 3), *pair(NZ, 3), *pair(NZ, 3), *pair(ITERS, 3),
+            pltpu.VMEM((2 * NZ, CH, HC), BF16),
+            pltpu.VMEM((2 * NZ, NX - 1, HALF, HC), BF16),
+            pltpu.VMEM((2 * NZ, CH, HC), BF16),
+            dma(3),
+            *pair(3), *pair(NZ, NY), *pair(NZ + 1), *pair(NZ, 3), *pair(NZ), *pair(NZ),
+            *pair(3), *pair(2, 3), *pair(NZ, 3), *pair(NZ, 3), *pair(2 * NZ, 3), *pair(2 * NZ, 3),
+            *pair(ITERS, 2, 3),
         ],
         compiler_params=pltpu.CompilerParams(
             collective_id=0, has_side_effects=True, vmem_limit_bytes=60 << 20
@@ -412,7 +519,7 @@
         name="adaround",
     )(
         tokens, weight, rounding, floor_codes,
-        scale_codes.reshape(1, COLS), zero_codes.reshape(1, COLS), kept,
+        scale_codes.reshape(1, COLS), zero_codes.reshape(1, COLS), block_mask,
     )
 
 

time: 173 us -> 162 us (0.936)
  Pallas kernels: 165 us -> 156 us
    pallas_call x1, Pallas kernels: 165 us -> 156 us  [per_device(): pl.pallas_call(kernel, out_shape=jax.ShapeDtypeStruct((FEAT, COLS), F32),...]
where the time goes in v3:
time: 162 us
  Pallas kernels  156 us (96%)
  local copies, waits for them, and re-layouts  5.39 us (3%)
    pallas_call x1, Pallas kernels, per_device(): pl.pallas_call(kernel, out_shape=jax.ShapeDtypeStruct((FEAT, COLS), F32),...  156 us

profile of v3, /device:TPU:2, one launch (start us, length us, event | category | flops | bytes accessed | tf_op | source)
XLA Modules:
  0.0 161.5 jit_solution(14150166122029671116)
XLA Ops:
  0.0 1.3 reshape.6.sc_ref
  1.3 1.3 reshape.7.zp_ref
  2.5 156.1 %adaround.1 = f32[512,896]{1,0:T(8,128)} custom-call(bf16[224,512]{1,0:T(8,128)(2,1)} %tok_ref.1, bf16[512,896]{1,0:T(8,128)(2,1)} %w_hbm.1, f32[512,896]{1,0:T(8,128)} %v_hbm.1, s32[512,896]{1,0:T(8,128)} %fc_hbm.1, s32[1,896]{1,0:T(1,128)} %reshape.6.sc_ref, s32[1,896]{1,0:T(1,128)} %reshape.7.zp_ref, s32[8,14]{1,0:T(8,128)} %mask_ref.1), custom_call_target="tpu_custom_call" | custom-call | flops 13153337344 | bytes 8388608 | tf_op jit(solution)/shard_map/adaround/pallas_call | solution.py:481
  158.7 2.8 %copy.9 = f32[512,896]{1,0:T(8,128)} copy(f32[512,896]{1,0:T(8,128)} %adaround.1) | data formatting | bytes 3670016

commit v4 on v3

--- a/solution.py
+++ b/solution.py
@@ -152,9 +152,9 @@
     def turn(ct, carry):
         c0 = pl.multiple_of(ct * 128, 128)
         cols = pl.ds(c0, 128)
-        scale = base_scale * jnp.exp2(sc_ref[:, cols].astype(F32) * 0.25)
-        sct[cols, :] = jnp.broadcast_to(scale, (128, 128)).T
-        zpt[cols, :] = jnp.broadcast_to(zp_ref[:, cols].astype(F32), (128, 128)).T
+        scale = base_scale * jnp.exp2(sc_ref[cols].astype(F32) * 0.25)
+        sct[cols, :] = jnp.broadcast_to(scale[None, :], (128, 128)).T
+        zpt[cols, :] = jnp.broadcast_to(zp_ref[cols].astype(F32)[None, :], (128, 128)).T
         for rt in range(FEAT // 128):
             rows = slice(rt * 128, rt * 128 + 128)
             vt[cols, rows] = v_ref[rows, cols].T
@@ -372,13 +372,17 @@
         partial_step(j)
 
     pairs = [(0,), (1, 2), (3, 4), (5, 6), (7,)]
+    ahead = {1: {0: 2, 2: 3}, 2: {0: 4}, 3: {}, 4: {}}
+    for j in pairs[1]:
+        gather_b(j)
     for k in range(1, 5):
         before, older = pairs[k - 1], pairs[k - 2] if k > 1 else ()
-        for j in pairs[k]:
-            gather_b(j)
         for d in range(NY):
             for j in pairs[k]:
                 gather_a(j, d)
+            if d in ahead[k]:
+                for j in pairs[ahead[k][d]]:
+                    gather_b(j)
             if d == 0:
                 for j in before:
                     sibling_step(j)
@@ -423,10 +427,10 @@
                 w2_copy(1, d).wait_recv()
 
         pl.when(s < 2 * NZ)(lambda: partial_two(s))
-        pl.when((s >= 2) & (s < 2 * NZ + 2))(lambda: sum_two(s - 2))
-        pl.when(s >= 4)(lambda: gradient_two(s - 4))
-
-        @pl.when(s == NZ + 3)
+        pl.when((s >= 4) & (s < 2 * NZ + 4))(lambda: sum_two(s - 4))
+        pl.when(s >= 8)(lambda: gradient_two(s - 8))
+
+        @pl.when(s == NZ + 7)
         def _():
             for d in (1, 2, 3):
                 g_copy(0, 0, d).wait_send()
@@ -434,7 +438,7 @@
 
         return carry
 
-    lax.fori_loop(0, 2 * NZ + 4, stage_two, 0)
+    lax.fori_loop(0, 2 * NZ + 8, stage_two, 0)
     for d in (1, 2, 3):
         g_copy(0, 1, d).wait_send()
     send_gradient(1, 1)
@@ -519,7 +523,7 @@
         name="adaround",
     )(
         tokens, weight, rounding, floor_codes,
-        scale_codes.reshape(1, COLS), zero_codes.reshape(1, COLS), block_mask,
+        scale_codes, zero_codes, block_mask,
     )
 
 

time: 162 us -> 156 us (0.963)
  Pallas kernels: 156 us -> 153 us
  local copies, waits for them, and re-layouts: 5.39 us -> 2.85 us
    pallas_call x1, Pallas kernels: 156 us -> 153 us  [per_device(): pl.pallas_call(kernel, out_shape=jax.ShapeDtypeStruct((FEAT, COLS), F32),...]
    reshape x2 -> x0, local copies, waits for them, and re-layouts: 2.55 us -> none  [the longest x1 1.28 us: per_device(): zero_codes.reshape(1, COLS)]
where the time goes in v4:
time: 156 us
  Pallas kernels  153 us (98%)
  local copies, waits for them, and re-layouts  2.85 us (2%)
    pallas_call x1, Pallas kernels, per_device(): pl.pallas_call(kernel, out_shape=jax.ShapeDtypeStruct((FEAT, COLS), F32),...  153 us

profile of v4, /device:TPU:2, one launch (start us, length us, event | category | flops | bytes accessed | tf_op | source)
XLA Modules:
  0.0 155.8 jit_solution(11555327347782178087)
XLA Ops:
  0.0 152.9 %adaround.1 = f32[512,896]{1,0:T(8,128)} custom-call(bf16[224,512]{1,0:T(8,128)(2,1)} %tok_ref.1, bf16[512,896]{1,0:T(8,128)(2,1)} %w_hbm.1, f32[512,896]{1,0:T(8,128)} %v_hbm.1, s32[512,896]{1,0:T(8,128)} %fc_hbm.1, s32[896]{0:T(1024)} %sc_ref.1, s32[896]{0:T(1024)} %zp_ref.1, s32[8,14]{1,0:T(8,128)} %mask_ref.1), custom_call_target="tpu_custom_call" | custom-call | flops 13153337344 | bytes 8388608 | tf_op jit(solution)/shard_map/adaround/pallas_call | solution.py:485
  152.9 2.8 %copy.9 = f32[512,896]{1,0:T(8,128)} copy(f32[512,896]{1,0:T(8,128)} %adaround.1) | data formatting | bytes 3670016

commit v5 on v4

--- a/solution.py
+++ b/solution.py
@@ -386,8 +386,6 @@
             if d == 0:
                 for j in before:
                     sibling_step(j)
-                for j in older:
-                    sum_step(j)
             if d == 1:
                 if k == 1:
                     for e in (1, 2, 3):
@@ -396,16 +394,18 @@
             if d == 2:
                 for j in before[1:]:
                     arrive(j)
+                for j in older:
+                    sum_step(j)
             if d == 3:
                 for j in pairs[k]:
                     sib(j, 0, (da_s, da_r)).start()
-                for j in older:
+                for j in pairs[k - 3] if k > 2 else ():
                     gradient_step(j)
     sibling_step(last)
     for j in pairs[3]:
         sum_step(j)
     arrive(last)
-    for j in pairs[3]:
+    for j in pairs[2] + pairs[3]:
         gradient_step(j)
     sum_step(last)
     gradient_step(last)
@@ -419,7 +419,7 @@
         w2_copy(0, d).wait_recv()
 
     def stage_two(s, carry):
-        pl.when(s == 2)(lambda: refine_half(1))
+        pl.when(s == 4)(lambda: refine_half(1))
 
         @pl.when(s == NZ)
         def _():
@@ -436,13 +436,13 @@
                 g_copy(0, 0, d).wait_send()
             send_gradient(1, 0)
 
+        pl.when(s == 2 * NZ + 3)(lambda: last_update(0))
         return carry
 
     lax.fori_loop(0, 2 * NZ + 8, stage_two, 0)
     for d in (1, 2, 3):
         g_copy(0, 1, d).wait_send()
     send_gradient(1, 1)
-    last_update(0)
     last_update(1)
 
     def turn_back(ct, carry):

time: 156 us -> 163 us (1.045)
  Pallas kernels: 153 us -> 159 us
    pallas_call x1, Pallas kernels: 153 us -> 159 us  [per_device(): pl.pallas_call(kernel, out_shape=jax.ShapeDtypeStruct((FEAT, COLS), F32),...]
where the time goes in v5:
time: 163 us; the launch traced here: 162 us
  Pallas kernels  159 us (98%)
  local copies, waits for them, and re-layouts  2.85 us (2%)
    pallas_call x1, Pallas kernels, per_device(): pl.pallas_call(kernel, out_shape=jax.ShapeDtypeStruct((FEAT, COLS), F32),...  159 us

profile of v5, /device:TPU:2, one launch (start us, length us, event | category | flops | bytes accessed | tf_op | source)
XLA Modules:
  0.0 161.9 jit_solution(3617585092339927338)
XLA Ops:
  0.0 159.1 %adaround.1 = f32[512,896]{1,0:T(8,128)} custom-call(bf16[224,512]{1,0:T(8,128)(2,1)} %tok_ref.1, bf16[512,896]{1,0:T(8,128)(2,1)} %w_hbm.1, f32[512,896]{1,0:T(8,128)} %v_hbm.1, s32[512,896]{1,0:T(8,128)} %fc_hbm.1, s32[896]{0:T(1024)} %sc_ref.1, s32[896]{0:T(1024)} %zp_ref.1, s32[8,14]{1,0:T(8,128)} %mask_ref.1), custom_call_target="tpu_custom_call" | custom-call | flops 13153337344 | bytes 8388608 | tf_op jit(solution)/shard_map/adaround/pallas_call | solution.py:485
  159.1 2.8 %copy.9 = f32[512,896]{1,0:T(8,128)} copy(f32[512,896]{1,0:T(8,128)} %adaround.1) | data formatting | bytes 3670016
